TPU v7x, 32 devices: a whole 2x2x4 slice. The times are simulated.
32 devices in a mesh: groups: 2 (over x), space: 16 (over z, y, core).
Axes of the slice: x: 2, y: 2, z: 4, core: 2. Of those that a mesh axis runs over, the one named last changes fastest.
Arguments:
- params: float32 [59, 262144], P(None, ('groups', 'space')), parts along dimension 1, may hold values from -6 to 3.2, as said below
- adam_m: float32 [59, 262144], P(None, ('groups', 'space')), parts along dimension 1, may hold values from -0.225 to 0.225
- adam_v: float32 [59, 262144], P(None, ('groups', 'space')), parts along dimension 1, may hold values from 5e-07 to 0.00045, as said below
- camera: float32 [12], P('groups'), parts along dimension 0, may hold values from -0.2 to 0.2
- target: float32 [256, 3, 256], P(('groups', 'space')), parts along dimension 0, may hold values from 0 to 1
- tile_ids: int32 [256], P(('groups', 'space')), parts along dimension 0, may hold values from 0 to 127, as said below
- tile_blocks: int32 [256], P(('groups', 'space')), parts along dimension 0, may hold values from 1 to 4, as said below
- tile_lists: int32 [256, 1024], P(('groups', 'space')), parts along dimension 0, may hold values from 0 to 8191, as said below
- send_rows: int32 [32, 16, 512], P(('groups', 'space')), parts along dimension 0, may hold values from 0 to 8191, as said below
Outputs:
- new_params: float32 [59, 262144], P(None, ('groups', 'space')), parts along dimension 1
- new_m: float32 [59, 262144], P(None, ('groups', 'space')), parts along dimension 1
- new_v: float32 [59, 262144], P(None, ('groups', 'space')), parts along dimension 1
There are 2 independent parts, one for each index of `groups`. A program takes and returns all parts, laid end to end along the dimension named above; each array names one. Nothing has to cross between parts.
Inputs may be any that keep to these rules, and one draw needn't show every extreme that they name: send_rows[s, d] names 512 distinct local columns of owner s, in the order in which renderer d receives them; no column of an owner goes to two renderers. `tile_ids`: a permutation of the 128 image tiles. `tile_blocks`: each tile slot lists 256 times this many Gaussians; one renderer, drawn from the seed, has all its tile slots at 4. `tile_lists`: each row holds distinct indices into the renderer's received columns; its first 256 times tile_blocks entries are live and ordered by increasing camera depth p_z, nearest Gaussian first; no received column is live in two tile slots of one renderer; entries at or after 256 times tile_blocks are ignored. `params`: attribute ranges: the position (attributes 0 to 2) lies within distance 3.2 of the anchor, log scale log 0.01 to log 0.06, rotation entries -1 to 1 with the first raised by 1.5, opacity logit -6 to -2.5, harmonics -0.9 to 0.9. `adam_v`: positive.
All inputs are finite; a program needn't handle non-finite values.
Results may differ from a plain program's by a relative error of at most 0.0003.
Values sent between devices are 32-bit elements; how exact they have to be, the bound alone decides.
A program may use at most 128 MiB of HBM per device.

v0:
```python
import jax
import jax.numpy as jnp
from jax import lax
from jax.sharding import PartitionSpec as P

BLOCK = 256
ADAM_STEP = 10


HIGHEST_PREC = lax.Precision.HIGHEST
BETA_ONE = 0.9
BETA_TWO = 0.999
ADAM_EPSILON = 1e-15
HARM_ZERO = 0.28209479177387814
HARM_ONE = 0.4886025119029199
HARM_TWO = (
    1.0925484305920792,
    -1.0925484305920792,
    0.31539156525252005,
    -1.0925484305920792,
    0.5462742152960396,
)
HARM_THREE = (
    -0.5900435899266435,
    2.890611442640554,
    -0.4570457994644658,
    0.3731763325901154,
    -0.4570457994644658,
    1.445305721320277,
    -0.5900435899266435,
)


def geometry(tiles_all):
    focal_len = max(256, tiles_all) * 5.0 / 3.0
    center_y = tiles_all * 0.5
    return (focal_len, center_y)


def rotation_of(camera):
    one_val = jnp.ones_like(camera[0])
    zero_val = jnp.zeros_like(camera[0])
    cos_a, sin_a = (jnp.cos(camera[0]), jnp.sin(camera[0]))
    cos_b, sin_b = (jnp.cos(camera[1]), jnp.sin(camera[1]))
    cos_c, sin_c = (jnp.cos(camera[2]), jnp.sin(camera[2]))
    around_x = jnp.stack(
        [
            jnp.stack([one_val, zero_val, zero_val]),
            jnp.stack([zero_val, cos_a, -sin_a]),
            jnp.stack([zero_val, sin_a, cos_a]),
        ]
    )
    around_y = jnp.stack(
        [
            jnp.stack([cos_b, zero_val, sin_b]),
            jnp.stack([zero_val, one_val, zero_val]),
            jnp.stack([-sin_b, zero_val, cos_b]),
        ]
    )
    around_z = jnp.stack(
        [
            jnp.stack([cos_c, -sin_c, zero_val]),
            jnp.stack([sin_c, cos_c, zero_val]),
            jnp.stack([zero_val, zero_val, one_val]),
        ]
    )
    return jnp.dot(
        around_z, jnp.dot(around_y, around_x, precision=HIGHEST_PREC), precision=HIGHEST_PREC
    )


def harmonic_basis(direction):
    dir_x, dir_y, dir_z = (direction[0], direction[1], direction[2])
    dir_xx, dir_yy, dir_zz = (dir_x * dir_x, dir_y * dir_y, dir_z * dir_z)
    terms = [
        HARM_ZERO * jnp.ones_like(dir_x),
        -HARM_ONE * dir_y,
        HARM_ONE * dir_z,
        -HARM_ONE * dir_x,
        HARM_TWO[0] * dir_x * dir_y,
        HARM_TWO[1] * dir_y * dir_z,
        HARM_TWO[2] * (2.0 * dir_zz - dir_xx - dir_yy),
        HARM_TWO[3] * dir_x * dir_z,
        HARM_TWO[4] * (dir_xx - dir_yy),
        HARM_THREE[0] * dir_y * (3.0 * dir_xx - dir_yy),
        HARM_THREE[1] * dir_x * dir_y * dir_z,
        HARM_THREE[2] * dir_y * (4.0 * dir_zz - dir_xx - dir_yy),
        HARM_THREE[3] * dir_z * (2.0 * dir_zz - 3.0 * dir_xx - 3.0 * dir_yy),
        HARM_THREE[4] * dir_x * (4.0 * dir_zz - dir_xx - dir_yy),
        HARM_THREE[5] * dir_z * (dir_xx - dir_yy),
        HARM_THREE[6] * dir_x * (dir_xx - 3.0 * dir_yy),
    ]
    return jnp.stack(terms)


def project(attr_rows, camera, focal_len, center_y):
    world_rot = rotation_of(camera)
    translate = jnp.stack([camera[3], camera[4], 5.0 + camera[5]])
    means = attr_rows[0:3]
    camera_space = jnp.dot(world_rot, means, precision=HIGHEST_PREC) + translate[:, None]
    inverse = 1.0 / camera_space[2]
    screen_u = focal_len * camera_space[0] * inverse + 128.0
    screen_v = focal_len * camera_space[1] * inverse + center_y
    scales = jnp.exp(attr_rows[3:6])
    quaternion = attr_rows[6:10] / jnp.sqrt(jnp.sum(attr_rows[6:10] * attr_rows[6:10], axis=0))
    q_r, q_x, q_y, q_z = (quaternion[0], quaternion[1], quaternion[2], quaternion[3])
    rotor = [
        [
            1.0 - 2.0 * (q_y * q_y + q_z * q_z),
            2.0 * (q_x * q_y - q_r * q_z),
            2.0 * (q_x * q_z + q_r * q_y),
        ],
        [
            2.0 * (q_x * q_y + q_r * q_z),
            1.0 - 2.0 * (q_x * q_x + q_z * q_z),
            2.0 * (q_y * q_z - q_r * q_x),
        ],
        [
            2.0 * (q_x * q_z - q_r * q_y),
            2.0 * (q_y * q_z + q_r * q_x),
            1.0 - 2.0 * (q_x * q_x + q_y * q_y),
        ],
    ]
    jac_zero = [focal_len * inverse, 0.0, -focal_len * camera_space[0] * inverse * inverse]
    jac_one = [0.0, focal_len * inverse, -focal_len * camera_space[1] * inverse * inverse]
    jacobian = [jac_zero, jac_one]
    mapped = []
    for outer in range(2):
        through = [
            sum((jacobian[outer][middle] * world_rot[middle, inner] for middle in range(3)))
            for inner in range(3)
        ]
        mapped.append(
            [
                sum((through[inner] * rotor[inner][column] for inner in range(3))) * scales[column]
                for column in range(3)
            ]
        )
    cov_aa = sum((mapped[0][column] * mapped[0][column] for column in range(3))) + 0.3
    cov_ab = sum((mapped[0][column] * mapped[1][column] for column in range(3)))
    cov_bb = sum((mapped[1][column] * mapped[1][column] for column in range(3))) + 0.3
    determinant = cov_aa * cov_bb - cov_ab * cov_ab
    opacity = jax.nn.sigmoid(attr_rows[10])
    centre = -jnp.dot(world_rot.T, translate, precision=HIGHEST_PREC)
    offset = means - centre[:, None]
    direction = offset / jnp.sqrt(jnp.sum(offset * offset, axis=0))
    harmonic = harmonic_basis(direction)
    coeffs = attr_rows[11:59].reshape(16, 3, attr_rows.shape[1])
    colour_rgb = jnp.maximum(jnp.sum(harmonic[:, None, :] * coeffs, axis=0) + 0.5, 0.0)
    firsts = jnp.stack(
        [
            screen_u,
            screen_v,
            cov_bb / determinant,
            -cov_ab / determinant,
            cov_aa / determinant,
            opacity,
        ]
    )
    return jnp.concatenate([firsts, colour_rgb], axis=0)


def tile_term(screen, tile_index, blocks, slots, target_tile):
    listed = jnp.take(screen, slots, axis=1)
    live_mask = (jnp.arange(slots.shape[0], dtype=jnp.int32) < blocks * BLOCK).astype(jnp.float32)
    pixels = jnp.arange(256, dtype=jnp.int32)
    pixel_x = (tile_index % 16 * 16 + pixels % 16).astype(jnp.float32)
    pixel_y = (tile_index // 16 * 16 + pixels // 16).astype(jnp.float32)
    delta_x = listed[0][None, :] - pixel_x[:, None]
    delta_y = listed[1][None, :] - pixel_y[:, None]
    exponent = (
        -0.5 * (listed[2][None, :] * delta_x * delta_x + listed[4][None, :] * delta_y * delta_y)
        - listed[3][None, :] * delta_x * delta_y
    )
    alphas = listed[5][None, :] * jnp.exp(exponent) * live_mask[None, :]
    log_keep = jnp.log1p(-alphas)
    before = jnp.cumsum(log_keep, axis=1) - log_keep
    weight = alphas * jnp.exp(before)
    render_rgb = jnp.einsum("cl,pl->cp", listed[6:9], weight, precision=HIGHEST_PREC)
    residual = render_rgb - target_tile
    return 0.5 * jnp.sum(residual * residual)


def render_loss(screen, tile_ids, tile_blocks, tile_lists, target):

    def per_tile(items):
        return tile_term(screen, items[0], items[1], items[2], items[3])

    terms = lax.map(jax.checkpoint(per_tile), (tile_ids, tile_blocks, tile_lists, target))
    return jnp.sum(terms)


def rate_table():
    return jnp.concatenate(
        [
            jnp.full((3,), 0.00016, jnp.float32),
            jnp.full((3,), 0.005, jnp.float32),
            jnp.full((4,), 0.001, jnp.float32),
            jnp.full((1,), 0.025, jnp.float32),
            jnp.full((3,), 0.0025, jnp.float32),
            jnp.full((45,), 0.000125, jnp.float32),
        ]
    )


def adam_update(params, adam_m, adam_v, param_grad):
    first_new = BETA_ONE * adam_m + (1.0 - BETA_ONE) * param_grad
    second_new = BETA_TWO * adam_v + (1.0 - BETA_TWO) * param_grad * param_grad
    fix_one = 1.0 - BETA_ONE**ADAM_STEP
    fix_two = 1.0 - BETA_TWO**ADAM_STEP
    stepped = first_new / fix_one / (jnp.sqrt(second_new / fix_two) + ADAM_EPSILON)
    return (params - rate_table()[:, None] * stepped, first_new, second_new)


def body(params, adam_m, adam_v, camera, target, tile_ids, tile_blocks, tile_lists, send_rows):
    spaces = lax.axis_size("space")
    focal_len, center_y = geometry(tile_ids.shape[0] * spaces)
    local_rows = send_rows[0].reshape(-1)
    capacity = send_rows.shape[2]
    picked = jnp.take(params, local_rows, axis=1)

    def local_loss(screen):
        return render_loss(screen, tile_ids, tile_blocks, tile_lists, target)

    def project_here(columns):
        return project(columns, camera, focal_len, center_y)

    arrived = lax.all_to_all(
        picked.reshape(picked.shape[0], spaces, capacity),
        "space",
        split_axis=1,
        concat_axis=1,
        tiled=True,
    )
    flat_rows = arrived.reshape(arrived.shape[0], spaces * capacity)

    def attribute_loss(columns):
        return local_loss(project_here(columns))

    gradient = jax.grad(attribute_loss)(flat_rows)
    returned = lax.all_to_all(
        gradient.reshape(gradient.shape[0], spaces, capacity),
        "space",
        split_axis=1,
        concat_axis=1,
        tiled=True,
    )
    picked_grad = returned.reshape(returned.shape[0], spaces * capacity)
    param_grad = jnp.zeros_like(params).at[:, local_rows].add(picked_grad)
    return adam_update(params, adam_m, adam_v, param_grad)


def solution(mesh):
    return jax.shard_map(
        body,
        mesh=mesh,
        in_specs=(
            P(None, ("groups", "space")),
            P(None, ("groups", "space")),
            P(None, ("groups", "space")),
            P("groups"),
            P(("groups", "space"), None, None),
            P(("groups", "space")),
            P(("groups", "space")),
            P(("groups", "space"), None),
            P(("groups", "space"), None, None),
        ),
        out_specs=(
            P(None, ("groups", "space")),
            P(None, ("groups", "space")),
            P(None, ("groups", "space")),
        ),
        check_vma=False,
    )
```

profile of v0, /device:TPU:1, one launch (start us, length us, event | category | flops | bytes accessed | tf_op | source)
XLA Modules:
  0.0 694.5 jit_solution(1190355153150540042)
XLA Ops:
  6.7 30.0 %gather_fusion.1 = f32[8192,59]{1,0:T(8,128)} fusion(f32[59,8192]{0,1:T(8,128)} %copy.149, s32[8192]{0:T(1024)S(1)} %broadcast_clamp_fusion.1), kind=kCustom, calls=%fused_computation.1 | custom fusion | bytes 3899392 | tf_op jit(solution)/shard_map/jit(_take)/gather | solution.py:220
  41.3 7.5 %all-to-all-start = ((f32[59,16,512]{2,0,1:T(8,128)}), f32[59,16,512]{2,0,1:T(8,128)S(1)}, u32[]{:S(2)}, u32[]{:S(2)}) async-start(f32[59,16,512]{2,0,1:T(8,128)} %broadcast_select_fusion), calls=%async_computation | async-start | bytes 4194304 | tf_op jit(solution)/shard_map/all_to_all | solution.py:228
  63.0 27.3 %all-to-all-done = f32[59,16,512]{2,0,1:T(8,128)S(1)} async-done(((f32[59,16,512]{2,0,1:T(8,128)}), f32[59,16,512]{2,0,1:T(8,128)S(1)}, u32[]{:S(2)}, u32[]{:S(2)}) %all-to-all-start) | async-done | bytes 1933344 | tf_op jit(solution)/shard_map/all_to_all | solution.py:228
  115.4 426.1 %while.15 = (s32[]{:T(128)}, f32[9,8192]{0,1:T(8,128)}, s32[8]{0:T(128)}, s32[8]{0:T(128)}, s32[8,1024]{1,0:T(8,128)}, /*index=5*/f32[8,3,256]{2,0,1:T(8,128)}, ...) while((s32[]{:T(128)}, f32[9,8192]{0,1:T(8,128)}, ...), condition=%wide.region_15.16_spmd, body=%wide.region_3.15_spmd.sunk | while | flops 125689624 | bytes 30528408 | solution.py:189
  123.7 5.0 gather_fusion
  159.3 9.7 %scatter_fusion = f32[9,8192]{0,1:T(8,128)} fusion(f32[9,8192]{0,1:T(8,128)} %get-tuple-element.496, s32[1024]{0:T(1024)} %get-tuple-element.456, f32[1024,9]{1,0:T(8,128)S(1)} %copy.237), kind=kCustom, calls=%fused_computation.2.clone.1 | custom fusion | flops 9216 | bytes 114688 | tf_op jit(solution)/shard_map/transpose(jvp())/while/body/eval_jaxpr/checkpoint/jit(_take)/scatter-add | solution.py:164
  176.9 5.0 gather_fusion
  212.5 9.7 %scatter_fusion = f32[9,8192]{0,1:T(8,128)} fusion(f32[9,8192]{0,1:T(8,128)} %get-tuple-element.496, s32[1024]{0:T(1024)} %get-tuple-element.456, f32[1024,9]{1,0:T(8,128)S(1)} %copy.237), kind=kCustom, calls=%fused_computation.2.clone.1 | custom fusion | flops 9216 | bytes 114688 | tf_op jit(solution)/shard_map/transpose(jvp())/while/body/eval_jaxpr/checkpoint/jit(_take)/scatter-add | solution.py:164
  230.1 5.0 gather_fusion
  265.7 9.7 %scatter_fusion = f32[9,8192]{0,1:T(8,128)} fusion(f32[9,8192]{0,1:T(8,128)} %get-tuple-element.496, s32[1024]{0:T(1024)} %get-tuple-element.456, f32[1024,9]{1,0:T(8,128)S(1)} %copy.237), kind=kCustom, calls=%fused_computation.2.clone.1 | custom fusion | flops 9216 | bytes 114688 | tf_op jit(solution)/shard_map/transpose(jvp())/while/body/eval_jaxpr/checkpoint/jit(_take)/scatter-add | solution.py:164
  283.3 5.0 gather_fusion
  318.9 9.7 %scatter_fusion = f32[9,8192]{0,1:T(8,128)} fusion(f32[9,8192]{0,1:T(8,128)} %get-tuple-element.496, s32[1024]{0:T(1024)} %get-tuple-element.456, f32[1024,9]{1,0:T(8,128)S(1)} %copy.237), kind=kCustom, calls=%fused_computation.2.clone.1 | custom fusion | flops 9216 | bytes 114688 | tf_op jit(solution)/shard_map/transpose(jvp())/while/body/eval_jaxpr/checkpoint/jit(_take)/scatter-add | solution.py:164
  336.5 5.0 gather_fusion
  372.0 9.7 %scatter_fusion = f32[9,8192]{0,1:T(8,128)} fusion(f32[9,8192]{0,1:T(8,128)} %get-tuple-element.496, s32[1024]{0:T(1024)} %get-tuple-element.456, f32[1024,9]{1,0:T(8,128)S(1)} %copy.237), kind=kCustom, calls=%fused_computation.2.clone.1 | custom fusion | flops 9216 | bytes 114688 | tf_op jit(solution)/shard_map/transpose(jvp())/while/body/eval_jaxpr/checkpoint/jit(_take)/scatter-add | solution.py:164
  389.6 5.0 gather_fusion
  425.2 9.7 %scatter_fusion = f32[9,8192]{0,1:T(8,128)} fusion(f32[9,8192]{0,1:T(8,128)} %get-tuple-element.496, s32[1024]{0:T(1024)} %get-tuple-element.456, f32[1024,9]{1,0:T(8,128)S(1)} %copy.237), kind=kCustom, calls=%fused_computation.2.clone.1 | custom fusion | flops 9216 | bytes 114688 | tf_op jit(solution)/shard_map/transpose(jvp())/while/body/eval_jaxpr/checkpoint/jit(_take)/scatter-add | solution.py:164
  442.8 5.0 gather_fusion
  478.4 9.7 %scatter_fusion = f32[9,8192]{0,1:T(8,128)} fusion(f32[9,8192]{0,1:T(8,128)} %get-tuple-element.496, s32[1024]{0:T(1024)} %get-tuple-element.456, f32[1024,9]{1,0:T(8,128)S(1)} %copy.237), kind=kCustom, calls=%fused_computation.2.clone.1 | custom fusion | flops 9216 | bytes 114688 | tf_op jit(solution)/shard_map/transpose(jvp())/while/body/eval_jaxpr/checkpoint/jit(_take)/scatter-add | solution.py:164
  496.0 5.0 gather_fusion
  531.6 9.7 %scatter_fusion = f32[9,8192]{0,1:T(8,128)} fusion(f32[9,8192]{0,1:T(8,128)} %get-tuple-element.496, s32[1024]{0:T(1024)} %get-tuple-element.456, f32[1024,9]{1,0:T(8,128)S(1)} %copy.237), kind=kCustom, calls=%fused_computation.2.clone.1 | custom fusion | flops 9216 | bytes 114688 | tf_op jit(solution)/shard_map/transpose(jvp())/while/body/eval_jaxpr/checkpoint/jit(_take)/scatter-add | solution.py:164
  563.6 5.9 fusion.93
  573.3 58.5 %all_to_all.10 = f32[59,16,512]{2,0,1:T(8,128)S(1)} all-to-all(f32[59,16,512]{2,0,1:T(8,128)S(1)} %copy.162), channel_id=1, replica_groups=mesh['groups'=2,'space'=16] {'space'}, dimensions={1} | all-to-all | bytes 3866624 | tf_op jit(solution)/shard_map/all_to_all | solution.py:241
  637.3 46.5 %scatter_custom_fusion.1 = f32[59,8192]{0,1:T(8,128)} fusion(s32[8192]{0:T(1024)} %bitcast.246, f32[8192,59]{1,0:T(8,128)} %copy.164, f32[]{:T(128)} %constant.280.clone.1), kind=kCustom, calls=%fused_computation.124 | custom fusion | flops 483328 | bytes 1933824 | tf_op jit(solution)/shard_map/scatter-add | solution.py:249
  687.8 6.4 multiply_subtract_fusion
  (801 shorter events, 350.9 us)
Async XLA Ops:
  41.3 12.7 %copy-start.84 = (f32[1,3]{1,0:T(1,128)S(1)}, f32[1,3]{1,0:T(1,128)}, u32[]{:S(2)}) copy-start(f32[1,3]{1,0:T(1,128)} %constant.288.clone.1) | copy-start | bytes 40
  41.3 12.7 %copy-start.85 = (f32[1,3]{1,0:T(1,128)S(1)}, f32[1,3]{1,0:T(1,128)}, u32[]{:S(2)}) copy-start(f32[1,3]{1,0:T(1,128)} %constant.289.clone.1) | copy-start | bytes 40
  41.3 12.8 %copy-start.83 = (f32[1,3]{1,0:T(1,128)S(1)}, f32[1,3]{1,0:T(1,128)}, u32[]{:S(2)}) copy-start(f32[1,3]{1,0:T(1,128)} %constant.287.clone.1) | copy-start | bytes 40
  41.3 49.0 %all-to-all-start = ((f32[59,16,512]{2,0,1:T(8,128)}), f32[59,16,512]{2,0,1:T(8,128)S(1)}, u32[]{:S(2)}, u32[]{:S(2)}) async-start(f32[59,16,512]{2,0,1:T(8,128)} %broadcast_select_fusion), calls=%async_computation | async-start | bytes 4194304 | tf_op jit(solution)/shard_map/all_to_all | solution.py:228
  54.3 38.7 %copy-start.77 = (f32[3,3]{1,0:T(4,128)}, f32[3,3]{1,0:T(4,128)S(1)}, u32[]{:S(2)}) copy-start(f32[3,3]{1,0:T(4,128)S(1)} %fusion.96) | copy-start | bytes 112
  63.0 30.0 %copy-start.80 = (f32[3]{0:T(128)}, f32[3]{0:T(128)S(1)}, u32[]{:S(2)}) copy-start(f32[3]{0:T(128)S(1)} %fusion.67) | copy-start | bytes 40
  90.5 10.9 %copy-start.20 = (f32[3,16,512]{2,0,1:T(4,128)}, f32[3,16,512]{2,0,1:T(4,128)S(1)}, u32[]{:S(2)}) copy-start(f32[3,16,512]{2,0,1:T(4,128)S(1)} %get-tuple-element.327) | copy-start | bytes 294916
  91.7 16.7 %copy-start.17 = (f32[3,8192]{1,0:T(4,128)}, f32[3,8192]{1,0:T(4,128)S(1)}, u32[]{:S(2)}) copy-start(f32[3,8192]{1,0:T(4,128)S(1)} %convolution_add_fusion.1) | copy-start | bytes 294916
  102.7 10.3 %copy-start.5 = (f32[4,16,512]{2,0,1:T(4,128)}, f32[4,16,512]{2,0,1:T(4,128)S(1)}, u32[]{:S(2)}) copy-start(f32[4,16,512]{2,0,1:T(4,128)S(1)} %get-tuple-element.330) | copy-start | bytes 393220
  123.1 9.0 %copy-start.36 = (f32[256]{0:T(256)}, f32[256]{0:T(256)S(1)}, u32[]{:S(2)}) copy-start(f32[256]{0:T(256)S(1)} %get-tuple-element.458) | copy-start | bytes 3076 | tf_op jit(solution)/shard_map/transpose(jvp())/while
  123.1 9.0 %copy-start.39 = (f32[256]{0:T(256)}, f32[256]{0:T(256)S(1)}, u32[]{:S(2)}) copy-start(f32[256]{0:T(256)S(1)} %get-tuple-element.462) | copy-start | bytes 3076 | tf_op jit(solution)/shard_map/transpose(jvp())/while
  176.3 9.0 %copy-start.36 = (f32[256]{0:T(256)}, f32[256]{0:T(256)S(1)}, u32[]{:S(2)}) copy-start(f32[256]{0:T(256)S(1)} %get-tuple-element.458) | copy-start | bytes 3076 | tf_op jit(solution)/shard_map/transpose(jvp())/while
  229.5 9.0 %copy-start.36 = (f32[256]{0:T(256)}, f32[256]{0:T(256)S(1)}, u32[]{:S(2)}) copy-start(f32[256]{0:T(256)S(1)} %get-tuple-element.458) | copy-start | bytes 3076 | tf_op jit(solution)/shard_map/transpose(jvp())/while
  282.6 9.0 %copy-start.36 = (f32[256]{0:T(256)}, f32[256]{0:T(256)S(1)}, u32[]{:S(2)}) copy-start(f32[256]{0:T(256)S(1)} %get-tuple-element.458) | copy-start | bytes 3076 | tf_op jit(solution)/shard_map/transpose(jvp())/while
  282.7 9.0 %copy-start.39 = (f32[256]{0:T(256)}, f32[256]{0:T(256)S(1)}, u32[]{:S(2)}) copy-start(f32[256]{0:T(256)S(1)} %get-tuple-element.462) | copy-start | bytes 3076 | tf_op jit(solution)/shard_map/transpose(jvp())/while
  335.8 9.0 %copy-start.36 = (f32[256]{0:T(256)}, f32[256]{0:T(256)S(1)}, u32[]{:S(2)}) copy-start(f32[256]{0:T(256)S(1)} %get-tuple-element.458) | copy-start | bytes 3076 | tf_op jit(solution)/shard_map/transpose(jvp())/while
  335.8 9.0 %copy-start.39 = (f32[256]{0:T(256)}, f32[256]{0:T(256)S(1)}, u32[]{:S(2)}) copy-start(f32[256]{0:T(256)S(1)} %get-tuple-element.462) | copy-start | bytes 3076 | tf_op jit(solution)/shard_map/transpose(jvp())/while
  389.0 9.0 %copy-start.36 = (f32[256]{0:T(256)}, f32[256]{0:T(256)S(1)}, u32[]{:S(2)}) copy-start(f32[256]{0:T(256)S(1)} %get-tuple-element.458) | copy-start | bytes 3076 | tf_op jit(solution)/shard_map/transpose(jvp())/while
  442.2 9.0 %copy-start.36 = (f32[256]{0:T(256)}, f32[256]{0:T(256)S(1)}, u32[]{:S(2)}) copy-start(f32[256]{0:T(256)S(1)} %get-tuple-element.458) | copy-start | bytes 3076 | tf_op jit(solution)/shard_map/transpose(jvp())/while
  495.4 9.0 %copy-start.36 = (f32[256]{0:T(256)}, f32[256]{0:T(256)S(1)}, u32[]{:S(2)}) copy-start(f32[256]{0:T(256)S(1)} %get-tuple-element.458) | copy-start | bytes 3076 | tf_op jit(solution)/shard_map/transpose(jvp())/while
  495.4 9.0 %copy-start.39 = (f32[256]{0:T(256)}, f32[256]{0:T(256)S(1)}, u32[]{:S(2)}) copy-start(f32[256]{0:T(256)S(1)} %get-tuple-element.462) | copy-start | bytes 3076 | tf_op jit(solution)/shard_map/transpose(jvp())/while
  557.8 11.7 %copy-start.52 = (f32[2,4,8,128]{3,1,2,0:T(4,128)S(1)}, f32[2,4,8,128]{3,1,2,0:T(4,128)}, u32[]{:S(2)}) copy-start(f32[2,4,8,128]{3,1,2,0:T(4,128)} %copy-done.50) | copy-start | bytes 98308
  557.8 11.7 %copy-start.78 = (f32[3,3]{1,0:T(4,128)S(1)}, f32[3,3]{1,0:T(4,128)}, u32[]{:S(2)}) copy-start(f32[3,3]{1,0:T(4,128)} %copy-done.77) | copy-start | bytes 112
  558.8 11.4 %copy-start.21 = (f32[3,16,512]{2,0,1:T(4,128)S(1)}, f32[3,16,512]{2,0,1:T(4,128)}, u32[]{:S(2)}) copy-start(f32[3,16,512]{2,0,1:T(4,128)} %copy-done.20) | copy-start | bytes 294916
  (175 other events, 613.0 us)
where the time goes:
time: 707 us; the launch traced here: 694 us
  other arithmetic  272 us (38%)
  local copies, waits for them, and re-layouts  234 us (33%)
  blocking collectives  58.5 us (8%)
  matrix products  51.6 us (7%)
  loops' own time  29.4 us (4%)
  waiting for transfers between devices  27.3 us (4%)
  between operations  14.1 us (2%)
  starting transfers between devices  7.49 us (1%)
    scatter-add x8, other arithmetic, tile_term(): listed = jnp.take(screen, slots, axis=1)  78 us
    all_to_all x1, blocking collectives, body(): lax.all_to_all(gradient.reshape(gradient.shape[0], spaces, capacity), 'sp...  58.5 us
    another operation x48, other arithmetic  54.4 us
    dot_general x24, matrix products, tile_term(): jnp.einsum('cl,pl->cp', listed[6:9], weight, precision=HIGHEST_PREC)  50.3 us
    another operation x56, local copies, waits for them, and re-layouts  46.8 us
    scatter-add x1, other arithmetic, body(): param_grad = jnp.zeros_like(params).at[:, local_rows].add(picked_grad)  46.5 us
    gather x8, local copies, waits for them, and re-layouts, tile_term(): listed = jnp.take(screen, slots, axis=1)  39.9 us
    dynamic_slice x40, local copies, waits for them, and re-layouts, render_loss(): lax.map(jax.checkpoint(per_tile), (tile_ids, tile_blocks, tile_lists, tar...  36.8 us
  transfers between devices with their start and end apart: 1, of which 1 were waited for; matrix products, arithmetic and copies ran while one was open for 0% of the time, Pallas kernels for 0%

commit v1 on v0

v1 whole, which is shorter than its diff:
```python
import functools

import jax
import jax.numpy as jnp
from jax import lax
from jax.experimental import pallas as pl
from jax.experimental.pallas import tpu as pltpu
from jax.sharding import PartitionSpec as P

BLOCK = 256
ADAM_STEP = 10
BETA_ONE = 0.9
BETA_TWO = 0.999
ADAM_EPSILON = 1e-15
HARM_ZERO = 0.28209479177387814
HARM_ONE = 0.4886025119029199
HARM_TWO = (
    1.0925484305920792,
    -1.0925484305920792,
    0.31539156525252005,
    -1.0925484305920792,
    0.5462742152960396,
)
HARM_THREE = (
    -0.5900435899266435,
    2.890611442640554,
    -0.4570457994644658,
    0.3731763325901154,
    -0.4570457994644658,
    1.445305721320277,
    -0.5900435899266435,
)
ATTRS = 59
SCREEN = 9
CHUNK = 1024
LANES = 128
F32 = jnp.float32
BF16 = jnp.bfloat16
VMEM_LIMIT = 56 * 1024 * 1024


def view_of(cam_ref):
    def splat(index):
        return jnp.full((8, LANES), cam_ref[index], F32)

    cos_a, sin_a = jnp.cos(splat(0)), jnp.sin(splat(0))
    cos_b, sin_b = jnp.cos(splat(1)), jnp.sin(splat(1))
    cos_c, sin_c = jnp.cos(splat(2)), jnp.sin(splat(2))
    world = [
        [
            cos_c * cos_b,
            cos_c * sin_b * sin_a - sin_c * cos_a,
            cos_c * sin_b * cos_a + sin_c * sin_a,
        ],
        [
            sin_c * cos_b,
            sin_c * sin_b * sin_a + cos_c * cos_a,
            sin_c * sin_b * cos_a - cos_c * sin_a,
        ],
        [-sin_b, cos_b * sin_a, cos_b * cos_a],
    ]
    translate = [splat(3), splat(4), 5.0 + splat(5)]
    centre = [-sum(world[k][i] * translate[k] for k in range(3)) for i in range(3)]
    return [world[i][j] for i in range(3) for j in range(3)] + translate + centre


def harmonic_basis(dir_x, dir_y, dir_z):
    dir_xx, dir_yy, dir_zz = (dir_x * dir_x, dir_y * dir_y, dir_z * dir_z)
    return [
        jnp.full_like(dir_x, HARM_ZERO),
        -HARM_ONE * dir_y,
        HARM_ONE * dir_z,
        -HARM_ONE * dir_x,
        HARM_TWO[0] * dir_x * dir_y,
        HARM_TWO[1] * dir_y * dir_z,
        HARM_TWO[2] * (2.0 * dir_zz - dir_xx - dir_yy),
        HARM_TWO[3] * dir_x * dir_z,
        HARM_TWO[4] * (dir_xx - dir_yy),
        HARM_THREE[0] * dir_y * (3.0 * dir_xx - dir_yy),
        HARM_THREE[1] * dir_x * dir_y * dir_z,
        HARM_THREE[2] * dir_y * (4.0 * dir_zz - dir_xx - dir_yy),
        HARM_THREE[3] * dir_z * (2.0 * dir_zz - 3.0 * dir_xx - 3.0 * dir_yy),
        HARM_THREE[4] * dir_x * (4.0 * dir_zz - dir_xx - dir_yy),
        HARM_THREE[5] * dir_z * (dir_xx - dir_yy),
        HARM_THREE[6] * dir_x * (dir_xx - 3.0 * dir_yy),
    ]


def project(attr, view, focal_len, center_y):
    world = [view[0:3], view[3:6], view[6:9]]
    translate, centre = view[9:12], view[12:15]
    cam = [sum(world[i][k] * attr[k] for k in range(3)) + translate[i] for i in range(3)]
    inverse = 1.0 / cam[2]
    screen_u = focal_len * cam[0] * inverse + 128.0
    screen_v = focal_len * cam[1] * inverse + center_y
    scales = [jnp.exp(attr[3 + k]) for k in range(3)]
    norm = lax.rsqrt(sum(attr[6 + k] * attr[6 + k] for k in range(4)))
    q_r, q_x, q_y, q_z = [attr[6 + k] * norm for k in range(4)]
    rotor = [
        [
            1.0 - 2.0 * (q_y * q_y + q_z * q_z),
            2.0 * (q_x * q_y - q_r * q_z),
            2.0 * (q_x * q_z + q_r * q_y),
        ],
        [
            2.0 * (q_x * q_y + q_r * q_z),
            1.0 - 2.0 * (q_x * q_x + q_z * q_z),
            2.0 * (q_y * q_z - q_r * q_x),
        ],
        [
            2.0 * (q_x * q_z - q_r * q_y),
            2.0 * (q_y * q_z + q_r * q_x),
            1.0 - 2.0 * (q_x * q_x + q_y * q_y),
        ],
    ]
    near = focal_len * inverse
    far = [-near * cam[outer] * inverse for outer in range(2)]
    mapped = []
    for outer in range(2):
        through = [near * world[outer][k] + far[outer] * world[2][k] for k in range(3)]
        mapped.append(
            [sum(through[k] * rotor[k][col] for k in range(3)) * scales[col] for col in range(3)]
        )
    cov_aa = sum(mapped[0][col] * mapped[0][col] for col in range(3)) + 0.3
    cov_ab = sum(mapped[0][col] * mapped[1][col] for col in range(3))
    cov_bb = sum(mapped[1][col] * mapped[1][col] for col in range(3)) + 0.3
    over = 1.0 / (cov_aa * cov_bb - cov_ab * cov_ab)
    opacity = 1.0 / (1.0 + jnp.exp(-attr[10]))
    offset = [attr[k] - centre[k] for k in range(3)]
    length = lax.rsqrt(sum(offset[k] * offset[k] for k in range(3)))
    basis = harmonic_basis(*[offset[k] * length for k in range(3)])
    colour = [
        jnp.maximum(sum(basis[k] * attr[11 + 3 * k + c] for k in range(16)) + 0.5, 0.0)
        for c in range(3)
    ]
    return [screen_u, screen_v, cov_bb * over, -cov_ab * over, cov_aa * over, opacity] + colour


def split(value, parts):
    out = []
    for index in range(parts):
        piece = value.astype(BF16)
        out.append(piece)
        if index + 1 < parts:
            value = value - piece.astype(F32)
    return out


def low_one_hot(index):
    rows = lax.broadcasted_iota(jnp.int32, (LANES, index.shape[1]), 0)
    return jnp.where(rows == (index & (LANES - 1)), 1.0, 0.0)


def high_match(index, groups):
    rows = lax.broadcasted_iota(jnp.int32, (groups, index.shape[1]), 0)
    return rows == (index >> 7)


def gather_columns(pieces, index, groups):
    hot = low_one_hot(index).astype(BF16)
    count = pieces.shape[1] // LANES
    hots = jnp.concatenate([hot] * count, axis=0)
    picked = jnp.dot(pieces, hots, preferred_element_type=F32)
    match = high_match(index, groups)
    return [
        jnp.sum(
            jnp.where(match, picked[r * groups : (r + 1) * groups], 0.0), axis=0, keepdims=True
        )
        for r in range(SCREEN)
    ]


def scatter_columns(rows, index, groups):
    hot = low_one_hot(index).astype(BF16)
    match = jnp.where(high_match(index, groups), 1.0, 0.0).astype(BF16)
    total = None
    for piece in split(rows, 2):
        left = jnp.concatenate([piece[r : r + 1] * match for r in range(SCREEN)], axis=0)
        part = lax.dot_general(
            left, hot, (((1,), (1,)), ((), ())), preferred_element_type=F32
        )
        total = part if total is None else total + part
    return total


def owner_kernel(sizes, params_ref, cam_ref, rows_ref, out_ref, view_ref, attr_ref, screen_ref):
    spaces, capacity, groups, focal_len, center_y = sizes
    step = pl.program_id(0)

    @pl.when(step == 0)
    def _():
        for k, value in enumerate(view_of(cam_ref)):
            view_ref[k] = value

    for q in range(8):
        attr_ref[pl.ds(q, ATTRS, stride=8), :] = params_ref[:, q * LANES : (q + 1) * LANES]
    view = [view_ref[k] for k in range(15)]
    attr = [attr_ref[8 * k : 8 * k + 8, :] for k in range(ATTRS)]
    values = project(attr, view, focal_len, center_y)
    for r in range(SCREEN):
        screen_ref[pl.ds(pl.multiple_of(r * groups + step * 8, 8), 8), :] = values[r]

    @pl.when(step == pl.num_programs(0) - 1)
    def _():
        pieces = jnp.concatenate(split(screen_ref[...], 3), axis=1)

        def send(d, carry):
            got = gather_columns(pieces, rows_ref[pl.ds(d, 1), :], groups)
            out_ref[d] = jnp.concatenate(got, axis=0)
            return carry

        lax.fori_loop(0, spaces, send, 0)


def render_kernel(
    sizes,
    recv_ref,
    lists_ref,
    target_ref,
    ids_ref,
    blocks_ref,
    out_ref,
    pieces_ref,
    lines_ref,
    alpha_ref,
    weight_ref,
    total_ref,
):
    spaces, capacity, groups, tiles, length = sizes
    per = capacity // LANES
    for r in range(SCREEN):
        for s in range(spaces):
            for k in range(per):
                row = r * groups + s * per + k
                lines_ref[row : row + 1, :] = recv_ref[s, r : r + 1, k * LANES : (k + 1) * LANES]
    for k, piece in enumerate(split(lines_ref[...], 3)):
        pieces_ref[:, k * LANES : (k + 1) * LANES] = piece
    total_ref[...] = jnp.zeros_like(total_ref)

    earlier = lax.broadcasted_iota(jnp.int32, (BLOCK, BLOCK), 0)
    later = lax.broadcasted_iota(jnp.int32, (BLOCK, BLOCK), 1)
    before = jnp.where(earlier < later, 1.0, 0.0).astype(BF16)
    upto = jnp.where(earlier <= later, 1.0, 0.0).astype(BF16)
    pixel = lax.broadcasted_iota(jnp.int32, (8, 256), 1)
    which = lax.broadcasted_iota(jnp.int32, (8, 256), 0)
    local_x = (pixel % 16 - 8).astype(F32)
    local_y = (pixel // 16 - 8).astype(F32)
    power = jnp.where(which == 0, 1.0, 0.0)
    for row, term in enumerate(
        [local_x, local_y, local_x * local_x, local_x * local_y, local_y * local_y]
    ):
        power = jnp.where(which == row + 1, term, power)
    power = power.astype(BF16)
    offsets = (lax.broadcasted_iota(jnp.int32, (16, BLOCK), 0) - 8).astype(F32)

    def prefix(value, ones):
        high, low = split(value, 2)
        return jnp.dot(high, ones, preferred_element_type=F32) + jnp.dot(
            low, ones, preferred_element_type=F32
        )

    def tile(i, carry):
        tile_id = ids_ref[i]
        live = blocks_ref[i] * BLOCK
        index_row = lists_ref[pl.ds(i, 1), :]
        base_x = ((tile_id % 16) * 16 + 8).astype(F32)
        base_y = ((tile_id // 16) * 16 + 8).astype(F32)
        kept = []
        run = jnp.zeros((256, 1), F32)
        render = jnp.zeros((8, 256), F32)
        for b in range(length // BLOCK):
            cut = slice(b * BLOCK, (b + 1) * BLOCK)
            index = index_row[:, cut]
            got = gather_columns(pieces_ref[...], index, groups)
            spot = lax.broadcasted_iota(jnp.int32, (1, BLOCK), 1) + b * BLOCK
            shown = jnp.where(spot < live, got[5], 0.0)
            local_u = got[0] - base_x
            local_v = got[1] - base_y
            delta_x = local_u - offsets
            delta_y = local_v - offsets
            part_x = -0.5 * got[2] * delta_x * delta_x
            part_y = -0.5 * got[4] * delta_y * delta_y
            cross = -got[3] * delta_y
            alpha = jnp.concatenate(
                [
                    shown
                    * jnp.exp(
                        part_x + part_y[y : y + 1, :] + delta_x * cross[y : y + 1, :]
                    )
                    for y in range(16)
                ],
                axis=0,
            )
            keep = jnp.log(1.0 - alpha)
            ahead = prefix(keep, before) + run
            run = ahead[:, BLOCK - 1 :] + keep[:, BLOCK - 1 :]
            weight = alpha * jnp.exp(ahead)
            colour = jnp.concatenate(got[6:9] + [jnp.zeros((5, BLOCK), F32)], axis=0)
            alpha_ref[:, cut] = alpha
            weight_ref[:, cut] = weight
            high, low = split(weight, 2)
            col_high, col_low = split(colour, 2)
            nt = (((1,), (1,)), ((), ()))
            for left, right in ((col_high, high), (col_low, high), (col_high, low)):
                render = render + lax.dot_general(left, right, nt, preferred_element_type=F32)
            kept.append((index, got, local_u, local_v, col_high, col_low))

        residual = render - jnp.concatenate([target_ref[i], jnp.zeros((5, 256), F32)], axis=0)
        res_high, res_low = split(residual, 2)
        turned = residual.T
        turn_high, turn_low = split(turned, 2)
        whole = jnp.sum((render * residual).T, axis=1, keepdims=True)
        for b in range(length // BLOCK):
            cut = slice(b * BLOCK, (b + 1) * BLOCK)
            index, got, local_u, local_v, col_high, col_low = kept[b]
            alpha = alpha_ref[:, cut]
            weight = weight_ref[:, cut]
            slope = (
                jnp.dot(turn_high, col_high, preferred_element_type=F32)
                + jnp.dot(turn_low, col_high, preferred_element_type=F32)
                + jnp.dot(turn_high, col_low, preferred_element_type=F32)
            )
            moved = slope * weight
            rest = whole - prefix(moved, upto)
            whole = rest[:, BLOCK - 1 :]
            push = moved - rest * (alpha / (1.0 - alpha))
            high, low = split(push, 2)
            moment = jnp.dot(power, high, preferred_element_type=F32) + jnp.dot(
                power, low, preferred_element_type=F32
            )
            high, low = split(weight, 2)
            hue = (
                jnp.dot(res_high, high, preferred_element_type=F32)
                + jnp.dot(res_low, high, preferred_element_type=F32)
                + jnp.dot(res_high, low, preferred_element_type=F32)
            )
            m_0, m_x, m_y, m_xx, m_xy, m_yy = [moment[k : k + 1] for k in range(6)]
            s_x = local_u * m_0 - m_x
            s_y = local_v * m_0 - m_y
            s_xx = local_u * (local_u * m_0 - 2.0 * m_x) + m_xx
            s_yy = local_v * (local_v * m_0 - 2.0 * m_y) + m_yy
            s_xy = local_u * s_y - local_v * m_x + m_xy
            back = jnp.concatenate(
                [
                    -(got[2] * s_x + got[3] * s_y),
                    -(got[4] * s_y + got[3] * s_x),
                    -0.5 * s_xx,
                    -s_xy,
                    -0.5 * s_yy,
                    m_0 / got[5],
                    hue[0:3],
                ],
                axis=0,
            )
            total_ref[...] += scatter_columns(back, index, groups)
        return carry

    lax.fori_loop(0, tiles, tile, 0)
    for r in range(SCREEN):
        for s in range(spaces):
            for k in range(per):
                row = r * groups + s * per + k
                out_ref[s, r : r + 1, k * LANES : (k + 1) * LANES] = total_ref[row : row + 1, :]


def update_kernel(
    sizes,
    params_ref,
    m_ref,
    v_ref,
    cam_ref,
    rows_ref,
    back_ref,
    new_params_ref,
    new_m_ref,
    new_v_ref,
    view_ref,
    attr_ref,
    total_ref,
):
    spaces, capacity, groups, focal_len, center_y = sizes
    step = pl.program_id(0)

    @pl.when(step == 0)
    def _():
        for k, value in enumerate(view_of(cam_ref)):
            view_ref[k] = value
        total_ref[...] = jnp.zeros_like(total_ref)

        def add(d, carry):
            total_ref[...] += scatter_columns(back_ref[d], rows_ref[pl.ds(d, 1), :], groups)
            return carry

        lax.fori_loop(0, spaces, add, 0)

    for q in range(8):
        attr_ref[pl.ds(q, ATTRS, stride=8), :] = params_ref[:, q * LANES : (q + 1) * LANES]
    view = [view_ref[k] for k in range(15)]
    attr = [attr_ref[8 * k : 8 * k + 8, :] for k in range(ATTRS)]
    slopes = [
        total_ref[pl.ds(pl.multiple_of(r * groups + step * 8, 8), 8), :] for r in range(SCREEN)
    ]
    _, pull = jax.vjp(lambda a: project(a, view, focal_len, center_y), attr)
    (grads,) = pull(slopes)
    for k in range(ATTRS):
        attr_ref[8 * k : 8 * k + 8, :] = grads[k]

    row = lax.broadcasted_iota(jnp.int32, (ATTRS, LANES), 0)
    rate = jnp.full((ATTRS, LANES), 0.000125, F32)
    for end, value in ((14, 0.0025), (11, 0.025), (10, 0.001), (6, 0.005), (3, 0.00016)):
        rate = jnp.where(row < end, value, rate)
    rate = rate * (1.0 / (1.0 - BETA_ONE**ADAM_STEP))
    fix_two = 1.0 / (1.0 - BETA_TWO**ADAM_STEP)
    for q in range(8):
        cut = slice(q * LANES, (q + 1) * LANES)
        grad = attr_ref[pl.ds(q, ATTRS, stride=8), :]
        first = BETA_ONE * m_ref[:, cut] + (1.0 - BETA_ONE) * grad
        second = BETA_TWO * v_ref[:, cut] + (1.0 - BETA_TWO) * grad * grad
        new_m_ref[:, cut] = first
        new_v_ref[:, cut] = second
        new_params_ref[:, cut] = params_ref[:, cut] - rate * first / (
            jnp.sqrt(second * fix_two) + ADAM_EPSILON
        )


def body(params, adam_m, adam_v, camera, target, tile_ids, tile_blocks, tile_lists, send_rows):
    spaces, capacity = send_rows.shape[1:]
    tiles, length = tile_lists.shape
    count = params.shape[1]
    tiles_all = tiles * spaces
    focal_len, center_y = max(256, tiles_all) * 5.0 / 3.0, tiles_all * 0.5
    groups = count // LANES
    heard = spaces * capacity // LANES
    rows = send_rows[0]
    steps = count // CHUNK
    vmem = pl.BlockSpec(memory_space=pltpu.VMEM)
    smem = pl.BlockSpec(memory_space=pltpu.SMEM)
    chunk = pl.BlockSpec((ATTRS, CHUNK), lambda i: (0, i))
    limits = pltpu.CompilerParams(vmem_limit_bytes=VMEM_LIMIT)
    owner_sizes = (spaces, capacity, groups, focal_len, center_y)
    packet = jax.ShapeDtypeStruct((spaces, SCREEN, capacity), F32)

    outgoing = pl.pallas_call(
        functools.partial(owner_kernel, owner_sizes),
        grid=(steps,),
        in_specs=[chunk, smem, vmem],
        out_specs=vmem,
        out_shape=packet,
        scratch_shapes=[
            pltpu.VMEM((15, 8, LANES), F32),
            pltpu.VMEM((8 * ATTRS, LANES), F32),
            pltpu.VMEM((SCREEN * groups, LANES), F32),
        ],
        compiler_params=limits,
        name="project_and_pick",
    )(params, camera, rows)
    arrived = lax.all_to_all(outgoing, "space", split_axis=0, concat_axis=0, tiled=True)
    slopes = pl.pallas_call(
        functools.partial(render_kernel, (spaces, capacity, heard, tiles, length)),
        in_specs=[vmem, vmem, vmem, smem, smem],
        out_specs=vmem,
        out_shape=packet,
        scratch_shapes=[
            pltpu.VMEM((SCREEN * heard, 3 * LANES), BF16),
            pltpu.VMEM((SCREEN * heard, LANES), F32),
            pltpu.VMEM((256, length), F32),
            pltpu.VMEM((256, length), F32),
            pltpu.VMEM((SCREEN * heard, LANES), F32),
        ],
        compiler_params=limits,
        name="render_and_back",
    )(arrived, tile_lists, target, tile_ids, tile_blocks)
    returned = lax.all_to_all(slopes, "space", split_axis=0, concat_axis=0, tiled=True)
    whole = jax.ShapeDtypeStruct(params.shape, F32)
    return pl.pallas_call(
        functools.partial(update_kernel, owner_sizes),
        grid=(steps,),
        in_specs=[chunk, chunk, chunk, smem, vmem, vmem],
        out_specs=[chunk, chunk, chunk],
        out_shape=[whole, whole, whole],
        scratch_shapes=[
            pltpu.VMEM((15, 8, LANES), F32),
            pltpu.VMEM((8 * ATTRS, LANES), F32),
            pltpu.VMEM((SCREEN * groups, LANES), F32),
        ],
        compiler_params=limits,
        name="gradient_and_step",
    )(params, adam_m, adam_v, camera, rows, returned)


def solution(mesh):
    wide = P(None, ("groups", "space"))
    tiles = ("groups", "space")
    return jax.shard_map(
        lambda *args: tuple(body(*args)),
        mesh=mesh,
        in_specs=(
            wide,
            wide,
            wide,
            P("groups"),
            P(tiles, None, None),
            P(tiles),
            P(tiles),
            P(tiles, None),
            P(tiles, None, None),
        ),
        out_specs=(wide, wide, wide),
        check_vma=False,
    )
```

time: 707 us -> 114 us (0.16); the launches traced: 694 us -> 113 us
  other arithmetic: 272 us -> 0 us
  local copies, waits for them, and re-layouts: 234 us -> 1.43 us
  Pallas kernels: 0 us -> 71.3 us
  matrix products: 51.6 us -> 0 us
  blocking collectives: 58.5 us -> 18.7 us
  loops' own time: 29.4 us -> 0 us
  waiting for transfers between devices: 27.3 us -> 13.4 us
  between operations: 14.1 us -> 0.65 us
    scatter-add x9 -> x0, other arithmetic: 125 us -> none  [the longest x8 78 us: tile_term(): listed = jnp.take(screen, slots, axis=1)]
    gather x10 -> x0, local copies, waits for them, and re-layouts: 72.8 us -> none  [the longest x8 39.9 us: tile_term(): listed = jnp.take(screen, slots, axis=1)]
    pallas_call x0 -> x3, Pallas kernels: none -> 71.3 us  [the longest x1 41.3 us: body(): pl.pallas_call(functools.partial(render_kernel, (spaces, capacity, heard,...]
    another operation x52 -> x0, other arithmetic: 54.7 us -> none
    dot_general x29 -> x0, matrix products: 51.6 us -> none  [the longest x24 50.3 us: tile_term(): jnp.einsum('cl,pl->cp', listed[6:9], weight, precision=HIGHEST_PREC)]
    another operation x58 -> x0, local copies, waits for them, and re-layouts: 48.6 us -> none
    all_to_all x1, blocking collectives: 58.5 us -> 18.7 us  [body(): lax.all_to_all(slopes, 'space', split_axis=0, concat_axis=0, tiled=True)]
    dynamic_slice x40 -> x0, local copies, waits for them, and re-layouts: 36.8 us -> none  [render_loss(): lax.map(jax.checkpoint(per_tile), (tile_ids, tile_blocks, tile_lists, tar...]
  transfers between devices with their start and end apart: 1 -> 1, of which waited for: 1 -> 1; matrix products, arithmetic and copies ran while one was open for 0% -> 1% of each run, Pallas kernels for 0% -> 0%
where the time goes in v1:
time: 114 us; the launch traced here: 113 us
  Pallas kernels  71.3 us (63%)
  blocking collectives  18.7 us (16%)
  waiting for transfers between devices  13.4 us (12%)
  starting transfers between devices  7.35 us (6%)
  local copies, waits for them, and re-layouts  1.43 us (1%)
    pallas_call x1, Pallas kernels, body(): pl.pallas_call(functools.partial(render_kernel, (spaces, capacity, heard,...  41.3 us
    all_to_all x1, blocking collectives, body(): lax.all_to_all(slopes, 'space', split_axis=0, concat_axis=0, tiled=True)  18.7 us
    pallas_call x1, Pallas kernels, body(): pl.pallas_call(functools.partial(update_kernel, owner_sizes), grid=(steps...  16.7 us
    all_to_all x1, waiting for transfers between devices, body(): lax.all_to_all(outgoing, 'space', split_axis=0, concat_axis=0, tiled=True)  13.4 us
    pallas_call x1, Pallas kernels, body(): pl.pallas_call(functools.partial(owner_kernel, owner_sizes), grid=(steps,...  13.3 us
    all_to_all x1, starting transfers between devices, body(): lax.all_to_all(outgoing, 'space', split_axis=0, concat_axis=0, tiled=True)  7.35 us
  transfers between devices with their start and end apart: 1, of which 1 were waited for; matrix products, arithmetic and copies ran while one was open for 1% of the time, Pallas kernels for 0%

profile of v1, /device:TPU:1, one launch (start us, length us, event | category | flops | bytes accessed | tf_op | source)
XLA Modules:
  0.0 112.8 jit_solution(9928344208042362196)
XLA Ops:
  0.6 0.0 copy-start.1
  0.6 13.3 %project_and_pick.1 = f32[16,9,512]{2,1,0:T(8,128)} custom-call(f32[59,8192]{1,0:T(8,128)} %params_ref.3, f32[6]{0:T(128)} %cam_ref.3, s32[16,512]{1,0:T(8,128)} %bitcast.1), custom_call_target="tpu_custom_call" | custom-call | tf_op jit(solution)/shard_map/project_and_pick/pallas_call | solution.py:443
  13.9 7.3 %all-to-all-start = ((f32[16,9,512]{2,1,0:T(8,128)}), f32[16,9,512]{2,1,0:T(8,128)S(1)}, u32[]{:S(2)}, u32[]{:S(2)}) async-start(f32[16,9,512]{2,1,0:T(8,128)} %project_and_pick.1), calls=%async_computation | async-start | bytes 1048576 | tf_op jit(solution)/shard_map/all_to_all | solution.py:457
  21.3 0.0 copy-done.1
  21.3 0.6 copy.12.target_ref
  21.9 13.4 %all-to-all-done.recv_ref = f32[16,9,512]{2,1,0:T(8,128)S(1)} async-done(((f32[16,9,512]{2,1,0:T(8,128)}), f32[16,9,512]{2,1,0:T(8,128)S(1)}, u32[]{:S(2)}, u32[]{:S(2)}) %all-to-all-start) | async-done | bytes 294944 | tf_op jit(solution)/shard_map/all_to_all | solution.py:457
  35.3 0.0 copy-start
  35.4 0.8 copy-done
  36.1 41.3 %render_and_back.1 = f32[16,9,512]{2,1,0:T(8,128)} custom-call(f32[16,9,512]{2,1,0:T(8,128)} %copy-done, s32[8,1024]{1,0:T(8,128)} %lists_ref.1, f32[8,3,256]{2,1,0:T(4,128)} %copy.12.target_ref, s32[8]{0:T(128)} %ids_ref.1, s32[8]{0:T(128)} %blocks_ref.1), custom_call_target="tpu_custom_call" | custom-call | tf_op jit(solution)/shard_map/render_and_back/pallas_call | solution.py:458
  77.5 18.7 %all_to_all.10.back_ref = f32[16,9,512]{2,1,0:T(8,128)} all-to-all(f32[16,9,512]{2,1,0:T(8,128)} %render_and_back.1), channel_id=1, replica_groups=mesh['groups'=2,'space'=16] {'space'}, dimensions={0} | all-to-all | bytes 589824 | tf_op jit(solution)/shard_map/all_to_all | solution.py:473
  96.2 16.7 %gradient_and_step.1 = (f32[59,8192]{1,0:T(8,128)}, f32[59,8192]{1,0:T(8,128)}, f32[59,8192]{1,0:T(8,128)}) custom-call(f32[59,8192]{1,0:T(8,128)} %params_ref.3, f32[59,8192]{1,0:T(8,128)} %m_ref.1, f32[59,8192]{1,0:T(8,128)} %v_ref.1, f32[6]{0:T(128)} %cam_ref.3, s32[16,512]{1,0:T(8,128)} %bitcast.2, f32[16,9,512]{2,1,0:T(8,128)} %all_to_all.10.back_ref), custom_call_target="tpu_custom_call" | custom-call | tf_op jit(solution)/shard_map/gradient_and_step/pallas_call | solution.py:475
Async XLA Ops:
  0.6 20.6 %copy-start.1 = (f32[8,3,256]{2,0,1:T(8,128)S(1)}, f32[8,3,256]{2,0,1:T(8,128)}, u32[]{:S(2)}) copy-start(f32[8,3,256]{2,0,1:T(8,128)} %param.13) | copy-start | bytes 73732
  13.9 21.4 %all-to-all-start = ((f32[16,9,512]{2,1,0:T(8,128)}), f32[16,9,512]{2,1,0:T(8,128)S(1)}, u32[]{:S(2)}, u32[]{:S(2)}) async-start(f32[16,9,512]{2,1,0:T(8,128)} %project_and_pick.1), calls=%async_computation | async-start | bytes 1048576 | tf_op jit(solution)/shard_map/all_to_all | solution.py:457
  35.3 0.8 copy-start

commit v2 on v1

--- a/solution.py
+++ b/solution.py
@@ -183,8 +183,8 @@
     return total
 
 
-def owner_kernel(sizes, params_ref, cam_ref, rows_ref, out_ref, view_ref, attr_ref, screen_ref):
-    spaces, capacity, groups, focal_len, center_y = sizes
+def owner_kernel(sizes, params_ref, cam_ref, screen_ref, view_ref, attr_ref):
+    groups, focal_len, center_y = sizes
     step = pl.program_id(0)
 
     @pl.when(step == 0)
@@ -200,39 +200,139 @@
     for r in range(SCREEN):
         screen_ref[pl.ds(pl.multiple_of(r * groups + step * 8, 8), 8), :] = values[r]
 
-    @pl.when(step == pl.num_programs(0) - 1)
-    def _():
-        pieces = jnp.concatenate(split(screen_ref[...], 3), axis=1)
-
-        def send(d, carry):
-            got = gather_columns(pieces, rows_ref[pl.ds(d, 1), :], groups)
-            out_ref[d] = jnp.concatenate(got, axis=0)
-            return carry
-
-        lax.fori_loop(0, spaces, send, 0)
+
+def greet(spaces):
+    me = lax.axis_index("space")
+    barrier = pltpu.get_barrier_semaphore()
+
+    def signal(t, carry):
+        pl.semaphore_signal(
+            barrier,
+            inc=1,
+            device_id={"space": lax.rem(me + t, spaces)},
+            device_id_type=pl.DeviceIdType.MESH,
+        )
+        return carry
+
+    lax.fori_loop(1, spaces, signal, 0)
+    pl.semaphore_wait(barrier, spaces - 1)
+
+
+def packet_copy(kept_ref, land_ref, send_sem, recv_sem, source, target):
+    return pltpu.make_async_remote_copy(
+        src_ref=kept_ref.at[target],
+        dst_ref=land_ref.at[source],
+        send_sem=send_sem.at[target],
+        recv_sem=recv_sem.at[source],
+        device_id={"space": target},
+        device_id_type=pl.DeviceIdType.MESH,
+    )
+
+
+def send_kernel(
+    sizes, screen_ref, rows_ref, lines_ref, pieces_ref, kept_ref, land_ref, send_sem, recv_sem
+):
+    spaces, capacity, groups = sizes
+    per = capacity // LANES
+    heard = spaces * per
+    me = lax.axis_index("space")
+    for k, piece in enumerate(split(screen_ref[...], 3)):
+        pieces_ref[:, k * LANES : (k + 1) * LANES] = piece
+
+    def pick(d):
+        got = gather_columns(pieces_ref[...], rows_ref[pl.ds(d, 1), :], groups)
+        return jnp.concatenate(got, axis=0)
+
+    def unpack(s, packet):
+        for r in range(SCREEN):
+            for k in range(per):
+                lines_ref[pl.ds(r * heard + s * per + k, 1), :] = packet[
+                    r : r + 1, k * LANES : (k + 1) * LANES
+                ]
+
+    greet(spaces)
+
+    def send(t, carry):
+        d = lax.rem(me + t, spaces)
+        kept_ref[d] = pick(d)
+        packet_copy(kept_ref, land_ref, send_sem, recv_sem, me, d).start()
+        return carry
+
+    lax.fori_loop(1, spaces, send, 0)
+    unpack(me, pick(me))
+
+    def take(t, carry):
+        s = lax.rem(me + spaces - t, spaces)
+        packet_copy(kept_ref, land_ref, send_sem, recv_sem, s, s).wait_recv()
+        unpack(s, land_ref[s])
+        return carry
+
+    lax.fori_loop(1, spaces, take, 0)
+
+    def done(t, carry):
+        d = lax.rem(me + t, spaces)
+        packet_copy(kept_ref, land_ref, send_sem, recv_sem, me, d).wait_send()
+        return carry
+
+    lax.fori_loop(1, spaces, done, 0)
+
+
+def return_kernel(
+    sizes, slopes_ref, rows_ref, out_ref, kept_ref, land_ref, send_sem, recv_sem
+):
+    spaces, capacity, groups = sizes
+    per = capacity // LANES
+    heard = spaces * per
+    me = lax.axis_index("space")
+
+    def pack(d):
+        for r in range(SCREEN):
+            for k in range(per):
+                kept_ref[d, r : r + 1, k * LANES : (k + 1) * LANES] = slopes_ref[
+                    pl.ds(r * heard + d * per + k, 1), :
+                ]
+
+    greet(spaces)
+
+    def send(t, carry):
+        d = lax.rem(me + t, spaces)
+        pack(d)
+        packet_copy(kept_ref, land_ref, send_sem, recv_sem, me, d).start()
+        return carry
+
+    lax.fori_loop(1, spaces, send, 0)
+    pack(me)
+    out_ref[...] = scatter_columns(kept_ref[me], rows_ref[pl.ds(me, 1), :], groups)
+
+    def take(t, carry):
+        s = lax.rem(me + spaces - t, spaces)
+        packet_copy(kept_ref, land_ref, send_sem, recv_sem, s, s).wait_recv()
+        out_ref[...] += scatter_columns(land_ref[s], rows_ref[pl.ds(s, 1), :], groups)
+        return carry
+
+    lax.fori_loop(1, spaces, take, 0)
+
+    def done(t, carry):
+        d = lax.rem(me + t, spaces)
+        packet_copy(kept_ref, land_ref, send_sem, recv_sem, me, d).wait_send()
+        return carry
+
+    lax.fori_loop(1, spaces, done, 0)
 
 
 def render_kernel(
     sizes,
-    recv_ref,
+    lines_ref,
     lists_ref,
     target_ref,
     ids_ref,
     blocks_ref,
-    out_ref,
+    total_ref,
     pieces_ref,
-    lines_ref,
     alpha_ref,
     weight_ref,
-    total_ref,
 ):
-    spaces, capacity, groups, tiles, length = sizes
-    per = capacity // LANES
-    for r in range(SCREEN):
-        for s in range(spaces):
-            for k in range(per):
-                row = r * groups + s * per + k
-                lines_ref[row : row + 1, :] = recv_ref[s, r : r + 1, k * LANES : (k + 1) * LANES]
+    groups, tiles, length = sizes
     for k, piece in enumerate(split(lines_ref[...], 3)):
         pieces_ref[:, k * LANES : (k + 1) * LANES] = piece
     total_ref[...] = jnp.zeros_like(total_ref)
@@ -356,11 +456,6 @@
         return carry
 
     lax.fori_loop(0, tiles, tile, 0)
-    for r in range(SCREEN):
-        for s in range(spaces):
-            for k in range(per):
-                row = r * groups + s * per + k
-                out_ref[s, r : r + 1, k * LANES : (k + 1) * LANES] = total_ref[row : row + 1, :]
 
 
 def update_kernel(
@@ -369,29 +464,20 @@
     m_ref,
     v_ref,
     cam_ref,
-    rows_ref,
-    back_ref,
+    total_ref,
     new_params_ref,
     new_m_ref,
     new_v_ref,
     view_ref,
     attr_ref,
-    total_ref,
 ):
-    spaces, capacity, groups, focal_len, center_y = sizes
+    groups, focal_len, center_y = sizes
     step = pl.program_id(0)
 
     @pl.when(step == 0)
     def _():
         for k, value in enumerate(view_of(cam_ref)):
             view_ref[k] = value
-        total_ref[...] = jnp.zeros_like(total_ref)
-
-        def add(d, carry):
-            total_ref[...] += scatter_columns(back_ref[d], rows_ref[pl.ds(d, 1), :], groups)
-            return carry
-
-        lax.fori_loop(0, spaces, add, 0)
 
     for q in range(8):
         attr_ref[pl.ds(q, ATTRS, stride=8), :] = params_ref[:, q * LANES : (q + 1) * LANES]
@@ -437,55 +523,75 @@
     smem = pl.BlockSpec(memory_space=pltpu.SMEM)
     chunk = pl.BlockSpec((ATTRS, CHUNK), lambda i: (0, i))
     limits = pltpu.CompilerParams(vmem_limit_bytes=VMEM_LIMIT)
-    owner_sizes = (spaces, capacity, groups, focal_len, center_y)
-    packet = jax.ShapeDtypeStruct((spaces, SCREEN, capacity), F32)
-
-    outgoing = pl.pallas_call(
-        functools.partial(owner_kernel, owner_sizes),
+    view_sizes = (groups, focal_len, center_y)
+    move_sizes = (spaces, capacity, groups)
+    view_scratch = [pltpu.VMEM((15, 8, LANES), F32), pltpu.VMEM((8 * ATTRS, LANES), F32)]
+    move_scratch = [
+        pltpu.VMEM((spaces, SCREEN, capacity), F32),
+        pltpu.VMEM((spaces, SCREEN, capacity), F32),
+        pltpu.SemaphoreType.DMA((spaces,)),
+        pltpu.SemaphoreType.DMA((spaces,)),
+    ]
+
+    def moving(number):
+        return pltpu.CompilerParams(
+            vmem_limit_bytes=VMEM_LIMIT, collective_id=number, has_side_effects=True
+        )
+
+    owned = jax.ShapeDtypeStruct((SCREEN * groups, LANES), F32)
+    listed = jax.ShapeDtypeStruct((SCREEN * heard, LANES), F32)
+    screen = pl.pallas_call(
+        functools.partial(owner_kernel, view_sizes),
         grid=(steps,),
-        in_specs=[chunk, smem, vmem],
+        in_specs=[chunk, smem],
         out_specs=vmem,
-        out_shape=packet,
-        scratch_shapes=[
-            pltpu.VMEM((15, 8, LANES), F32),
-            pltpu.VMEM((8 * ATTRS, LANES), F32),
-            pltpu.VMEM((SCREEN * groups, LANES), F32),
-        ],
+        out_shape=owned,
+        scratch_shapes=view_scratch,
         compiler_params=limits,
-        name="project_and_pick",
-    )(params, camera, rows)
-    arrived = lax.all_to_all(outgoing, "space", split_axis=0, concat_axis=0, tiled=True)
+        name="project",
+    )(params, camera)
+    arrived = pl.pallas_call(
+        functools.partial(send_kernel, move_sizes),
+        in_specs=[vmem, vmem],
+        out_specs=vmem,
+        out_shape=listed,
+        scratch_shapes=[pltpu.VMEM((SCREEN * groups, 3 * LANES), BF16)] + move_scratch,
+        compiler_params=moving(0),
+        name="pick_and_send",
+    )(screen, rows)
     slopes = pl.pallas_call(
-        functools.partial(render_kernel, (spaces, capacity, heard, tiles, length)),
+        functools.partial(render_kernel, (heard, tiles, length)),
         in_specs=[vmem, vmem, vmem, smem, smem],
         out_specs=vmem,
-        out_shape=packet,
+        out_shape=listed,
         scratch_shapes=[
             pltpu.VMEM((SCREEN * heard, 3 * LANES), BF16),
-            pltpu.VMEM((SCREEN * heard, LANES), F32),
             pltpu.VMEM((256, length), F32),
             pltpu.VMEM((256, length), F32),
-            pltpu.VMEM((SCREEN * heard, LANES), F32),
         ],
         compiler_params=limits,
         name="render_and_back",
     )(arrived, tile_lists, target, tile_ids, tile_blocks)
-    returned = lax.all_to_all(slopes, "space", split_axis=0, concat_axis=0, tiled=True)
+    total = pl.pallas_call(
+        functools.partial(return_kernel, move_sizes),
+        in_specs=[vmem, vmem],
+        out_specs=vmem,
+        out_shape=owned,
+        scratch_shapes=move_scratch,
+        compiler_params=moving(1),
+        name="return_and_add",
+    )(slopes, rows)
     whole = jax.ShapeDtypeStruct(params.shape, F32)
     return pl.pallas_call(
-        functools.partial(update_kernel, owner_sizes),
+        functools.partial(update_kernel, view_sizes),
         grid=(steps,),
-        in_specs=[chunk, chunk, chunk, smem, vmem, vmem],
+        in_specs=[chunk, chunk, chunk, smem, vmem],
         out_specs=[chunk, chunk, chunk],
         out_shape=[whole, whole, whole],
-        scratch_shapes=[
-            pltpu.VMEM((15, 8, LANES), F32),
-            pltpu.VMEM((8 * ATTRS, LANES), F32),
-            pltpu.VMEM((SCREEN * groups, LANES), F32),
-        ],
+        scratch_shapes=view_scratch,
         compiler_params=limits,
         name="gradient_and_step",
-    )(params, adam_m, adam_v, camera, rows, returned)
+    )(params, adam_m, adam_v, camera, total)
 
 
 def solution(mesh):

time: 114 us -> 98.9 us (0.87)
  Pallas kernels: 71.3 us -> 95.5 us
  blocking collectives: 18.7 us -> 0 us
  waiting for transfers between devices: 13.4 us -> 0 us
  starting transfers between devices: 7.35 us -> 0 us
    pallas_call x3 -> x5, Pallas kernels: 71.3 us -> 95.5 us  [the longest x1 40.7 us: body(): pl.pallas_call(functools.partial(render_kernel, (heard, tiles, length)),...]
    all_to_all x1 -> x0, blocking collectives: 18.7 us -> none  [body(): lax.all_to_all(slopes, 'space', split_axis=0, concat_axis=0, tiled=True)]
    all_to_all x1 -> x0, waiting for transfers between devices: 13.4 us -> none  [body(): lax.all_to_all(outgoing, 'space', split_axis=0, concat_axis=0, tiled=True)]
    all_to_all x1 -> x0, starting transfers between devices: 7.35 us -> none  [body(): lax.all_to_all(outgoing, 'space', split_axis=0, concat_axis=0, tiled=True)]
  transfers between devices with their start and end apart: 1 -> 0, of which waited for: 1 -> 0; matrix products, arithmetic and copies ran while one was open for 1% -> 0% of each run, Pallas kernels for 0% -> 0%
where the time goes in v2:
time: 98.9 us; the launch traced here: 97.5 us
  Pallas kernels  95.5 us (97%)
  local copies, waits for them, and re-layouts  1.37 us (1%)
    pallas_call x1, Pallas kernels, body(): pl.pallas_call(functools.partial(render_kernel, (heard, tiles, length)),...  40.7 us
    pallas_call x1, Pallas kernels, body(): pl.pallas_call(functools.partial(return_kernel, move_sizes), in_specs=[vm...  20.9 us
    pallas_call x1, Pallas kernels, body(): pl.pallas_call(functools.partial(send_kernel, move_sizes), in_specs=[vmem...  19.7 us
    pallas_call x1, Pallas kernels, body(): pl.pallas_call(functools.partial(update_kernel, view_sizes), grid=(steps,...  8.91 us
    pallas_call x1, Pallas kernels, body(): pl.pallas_call(functools.partial(owner_kernel, view_sizes), grid=(steps,)...  5.29 us

profile of v2, /device:TPU:1, one launch (start us, length us, event | category | flops | bytes accessed | tf_op | source)
XLA Modules:
  0.0 97.5 jit_solution(16605343104960001915)
XLA Ops:
  0.6 1.4 %copy.12.target_ref = f32[8,3,256]{2,1,0:T(4,128)} copy(f32[8,3,256]{2,0,1:T(8,128)} %param.13) | data formatting | bytes 49152 | tf_op args[4]
  2.0 5.3 %project.1.screen_ref = f32[576,128]{1,0:T(8,128)} custom-call(f32[59,8192]{1,0:T(8,128)} %params_ref.3, f32[6]{0:T(128)} %cam_ref.3), custom_call_target="tpu_custom_call" | custom-call | tf_op jit(solution)/shard_map/project/pallas_call | solution.py:543
  7.3 19.7 %pick_and_send.1.lines_ref = f32[576,128]{1,0:T(8,128)} custom-call(f32[576,128]{1,0:T(8,128)} %project.1.screen_ref, s32[16,512]{1,0:T(8,128)} %bitcast.1), custom_call_target="tpu_custom_call" | custom-call | tf_op jit(solution)/shard_map/pick_and_send/pallas_call | solution.py:553
  27.0 40.7 %render_and_back.1.slopes_ref = f32[576,128]{1,0:T(8,128)} custom-call(f32[576,128]{1,0:T(8,128)} %pick_and_send.1.lines_ref, s32[8,1024]{1,0:T(8,128)} %lists_ref.1, f32[8,3,256]{2,1,0:T(4,128)} %copy.12.target_ref, s32[8]{0:T(128)} %ids_ref.1, s32[8]{0:T(128)} %blocks_ref.1), custom_call_target="tpu_custom_call" | custom-call | tf_op jit(solution)/shard_map/render_and_back/pallas_call | solution.py:562
  67.7 20.9 %return_and_add.1.total_ref = f32[576,128]{1,0:T(8,128)} custom-call(f32[576,128]{1,0:T(8,128)} %render_and_back.1.slopes_ref, s32[16,512]{1,0:T(8,128)} %bitcast.2), custom_call_target="tpu_custom_call" | custom-call | tf_op jit(solution)/shard_map/return_and_add/pallas_call | solution.py:575
  88.6 8.9 %gradient_and_step.1 = (f32[59,8192]{1,0:T(8,128)}, f32[59,8192]{1,0:T(8,128)}, f32[59,8192]{1,0:T(8,128)}) custom-call(f32[59,8192]{1,0:T(8,128)} %params_ref.3, f32[59,8192]{1,0:T(8,128)} %m_ref.1, f32[59,8192]{1,0:T(8,128)} %v_ref.1, f32[6]{0:T(128)} %cam_ref.3, f32[576,128]{1,0:T(8,128)} %return_and_add.1.total_ref), custom_call_target="tpu_custom_call" | custom-call | tf_op jit(solution)/shard_map/gradient_and_step/pallas_call | solution.py:585

commit v3 on v2

--- a/solution.py
+++ b/solution.py
@@ -34,6 +34,7 @@
 SCREEN = 9
 CHUNK = 1024
 LANES = 128
+WIDE = 256
 F32 = jnp.float32
 BF16 = jnp.bfloat16
 VMEM_LIMIT = 56 * 1024 * 1024
@@ -147,31 +148,43 @@
 
 
 def low_one_hot(index):
-    rows = lax.broadcasted_iota(jnp.int32, (LANES, index.shape[1]), 0)
-    return jnp.where(rows == (index & (LANES - 1)), 1.0, 0.0)
+    rows = lax.broadcasted_iota(jnp.int32, (WIDE, index.shape[1]), 0)
+    return jnp.where(rows == (index & (WIDE - 1)), 1.0, 0.0).astype(BF16)
 
 
 def high_match(index, groups):
     rows = lax.broadcasted_iota(jnp.int32, (groups, index.shape[1]), 0)
-    return rows == (index >> 7)
-
-
-def gather_columns(pieces, index, groups):
-    hot = low_one_hot(index).astype(BF16)
-    count = pieces.shape[1] // LANES
-    hots = jnp.concatenate([hot] * count, axis=0)
-    picked = jnp.dot(pieces, hots, preferred_element_type=F32)
+    return rows == (index >> 8)
+
+
+def store_pieces(lines_ref, pieces_ref):
+    main = lines_ref.shape[0] // 2
+    groups = main // SCREEN
+    for half in range(2):
+        parts = split(lines_ref[pl.ds(half, main, stride=2), :], 3)
+        for k in range(2):
+            start = k * WIDE + half * LANES
+            pieces_ref[0:main, start : start + LANES] = parts[k]
+        pieces_ref[main:, half * LANES : (half + 1) * LANES] = parts[2][0 : 2 * groups]
+    pieces_ref[main:, WIDE:] = jnp.zeros((2 * groups, WIDE), BF16)
+
+
+def gather_columns(pieces, index, hot):
+    groups = pieces.shape[0] // (SCREEN + 2)
+    picked = jnp.dot(
+        pieces, jnp.concatenate([hot, hot], axis=0), preferred_element_type=F32
+    )
     match = high_match(index, groups)
-    return [
-        jnp.sum(
-            jnp.where(match, picked[r * groups : (r + 1) * groups], 0.0), axis=0, keepdims=True
-        )
-        for r in range(SCREEN)
-    ]
-
-
-def scatter_columns(rows, index, groups):
-    hot = low_one_hot(index).astype(BF16)
+    out = []
+    for r in range(SCREEN):
+        value = picked[r * groups : (r + 1) * groups]
+        if r < 2:
+            value = value + picked[(SCREEN + r) * groups : (SCREEN + r + 1) * groups]
+        out.append(jnp.sum(jnp.where(match, value, 0.0), axis=0, keepdims=True))
+    return out
+
+
+def scatter_columns(rows, index, hot, groups):
     match = jnp.where(high_match(index, groups), 1.0, 0.0).astype(BF16)
     total = None
     for piece in split(rows, 2):
@@ -183,6 +196,13 @@
     return total
 
 
+def store_lines(lines_ref, wide):
+    for half in range(2):
+        lines_ref[pl.ds(half, wide.shape[0], stride=2), :] = wide[
+            :, half * LANES : (half + 1) * LANES
+        ]
+
+
 def owner_kernel(sizes, params_ref, cam_ref, screen_ref, view_ref, attr_ref):
     groups, focal_len, center_y = sizes
     step = pl.program_id(0)
@@ -236,11 +256,11 @@
     per = capacity // LANES
     heard = spaces * per
     me = lax.axis_index("space")
-    for k, piece in enumerate(split(screen_ref[...], 3)):
-        pieces_ref[:, k * LANES : (k + 1) * LANES] = piece
+    store_pieces(screen_ref, pieces_ref)
 
     def pick(d):
-        got = gather_columns(pieces_ref[...], rows_ref[pl.ds(d, 1), :], groups)
+        index = rows_ref[pl.ds(d, 1), :]
+        got = gather_columns(pieces_ref[...], index, low_one_hot(index))
         return jnp.concatenate(got, axis=0)
 
     def unpack(s, packet):
@@ -278,7 +298,7 @@
 
 
 def return_kernel(
-    sizes, slopes_ref, rows_ref, out_ref, kept_ref, land_ref, send_sem, recv_sem
+    sizes, slopes_ref, rows_ref, out_ref, total_ref, kept_ref, land_ref, send_sem, recv_sem
 ):
     spaces, capacity, groups = sizes
     per = capacity // LANES
@@ -302,15 +322,21 @@
 
     lax.fori_loop(1, spaces, send, 0)
     pack(me)
-    out_ref[...] = scatter_columns(kept_ref[me], rows_ref[pl.ds(me, 1), :], groups)
+
+    def spread(packet, s):
+        index = rows_ref[pl.ds(s, 1), :]
+        return scatter_columns(packet, index, low_one_hot(index), groups // 2)
+
+    total_ref[...] = spread(kept_ref[me], me)
 
     def take(t, carry):
         s = lax.rem(me + spaces - t, spaces)
         packet_copy(kept_ref, land_ref, send_sem, recv_sem, s, s).wait_recv()
-        out_ref[...] += scatter_columns(land_ref[s], rows_ref[pl.ds(s, 1), :], groups)
+        total_ref[...] += spread(land_ref[s], s)
         return carry
 
     lax.fori_loop(1, spaces, take, 0)
+    store_lines(out_ref, total_ref[...])
 
     def done(t, carry):
         d = lax.rem(me + t, spaces)
@@ -327,20 +353,23 @@
     target_ref,
     ids_ref,
     blocks_ref,
+    out_ref,
     total_ref,
     pieces_ref,
-    alpha_ref,
-    weight_ref,
+    high_ref,
+    low_ref,
+    ratio_ref,
 ):
     groups, tiles, length = sizes
-    for k, piece in enumerate(split(lines_ref[...], 3)):
-        pieces_ref[:, k * LANES : (k + 1) * LANES] = piece
+    store_pieces(lines_ref, pieces_ref)
     total_ref[...] = jnp.zeros_like(total_ref)
 
     earlier = lax.broadcasted_iota(jnp.int32, (BLOCK, BLOCK), 0)
     later = lax.broadcasted_iota(jnp.int32, (BLOCK, BLOCK), 1)
     before = jnp.where(earlier < later, 1.0, 0.0).astype(BF16)
+    before = jnp.concatenate([before, before], axis=0)
     upto = jnp.where(earlier <= later, 1.0, 0.0).astype(BF16)
+    upto = jnp.concatenate([upto, upto], axis=0)
     pixel = lax.broadcasted_iota(jnp.int32, (8, 256), 1)
     which = lax.broadcasted_iota(jnp.int32, (8, 256), 0)
     local_x = (pixel % 16 - 8).astype(F32)
@@ -354,12 +383,14 @@
     offsets = (lax.broadcasted_iota(jnp.int32, (16, BLOCK), 0) - 8).astype(F32)
 
     def prefix(value, ones):
-        high, low = split(value, 2)
-        return jnp.dot(high, ones, preferred_element_type=F32) + jnp.dot(
-            low, ones, preferred_element_type=F32
+        return jnp.dot(
+            jnp.concatenate(split(value, 2), axis=1), ones, preferred_element_type=F32
         )
 
-    def tile(i, carry):
+    def both(high, low):
+        return jnp.concatenate([high.astype(F32), low.astype(F32)], axis=0).astype(BF16)
+
+    def front(i, slot):
         tile_id = ids_ref[i]
         live = blocks_ref[i] * BLOCK
         index_row = lists_ref[pl.ds(i, 1), :]
@@ -369,9 +400,10 @@
         run = jnp.zeros((256, 1), F32)
         render = jnp.zeros((8, 256), F32)
         for b in range(length // BLOCK):
-            cut = slice(b * BLOCK, (b + 1) * BLOCK)
-            index = index_row[:, cut]
-            got = gather_columns(pieces_ref[...], index, groups)
+            index = index_row[:, b * BLOCK : (b + 1) * BLOCK]
+            cut = slice(slot * length + b * BLOCK, slot * length + (b + 1) * BLOCK)
+            hot = low_one_hot(index)
+            got = gather_columns(pieces_ref[...], index, hot)
             spot = lax.broadcasted_iota(jnp.int32, (1, BLOCK), 1) + b * BLOCK
             shown = jnp.where(spot < live, got[5], 0.0)
             local_u = got[0] - base_x
@@ -396,44 +428,46 @@
             run = ahead[:, BLOCK - 1 :] + keep[:, BLOCK - 1 :]
             weight = alpha * jnp.exp(ahead)
             colour = jnp.concatenate(got[6:9] + [jnp.zeros((5, BLOCK), F32)], axis=0)
-            alpha_ref[:, cut] = alpha
-            weight_ref[:, cut] = weight
+            over = pl.reciprocal(1.0 - alpha, approx=True)
+            over = over * (2.0 - (1.0 - alpha) * over)
+            ratio_ref[:, cut] = alpha * over
             high, low = split(weight, 2)
+            high_ref[:, cut] = high
+            low_ref[:, cut] = low
             col_high, col_low = split(colour, 2)
             nt = (((1,), (1,)), ((), ()))
-            for left, right in ((col_high, high), (col_low, high), (col_high, low)):
-                render = render + lax.dot_general(left, right, nt, preferred_element_type=F32)
-            kept.append((index, got, local_u, local_v, col_high, col_low))
-
+            stacked = both(col_high, col_low)
+            part = lax.dot_general(stacked, high, nt, preferred_element_type=F32)
+            render = render + part[0:8] + part[8:16]
+            render = render + lax.dot_general(col_high, low, nt, preferred_element_type=F32)
+            kept.append((index, hot, got, local_u, local_v))
+        return render, kept
+
+    def rear(i, slot, render, kept):
         residual = render - jnp.concatenate([target_ref[i], jnp.zeros((5, 256), F32)], axis=0)
         res_high, res_low = split(residual, 2)
-        turned = residual.T
-        turn_high, turn_low = split(turned, 2)
-        whole = jnp.sum((render * residual).T, axis=1, keepdims=True)
+        res_both = both(res_high, res_low)
+        whole = jnp.sum(render * residual, axis=0, keepdims=True)
+        turned = jnp.concatenate([residual[0:3], whole, residual[4:8]], axis=0).T
+        red, green, blue, whole = [turned[:, k : k + 1] for k in range(4)]
         for b in range(length // BLOCK):
-            cut = slice(b * BLOCK, (b + 1) * BLOCK)
-            index, got, local_u, local_v, col_high, col_low = kept[b]
-            alpha = alpha_ref[:, cut]
-            weight = weight_ref[:, cut]
-            slope = (
-                jnp.dot(turn_high, col_high, preferred_element_type=F32)
-                + jnp.dot(turn_low, col_high, preferred_element_type=F32)
-                + jnp.dot(turn_high, col_low, preferred_element_type=F32)
-            )
+            cut = slice(slot * length + b * BLOCK, slot * length + (b + 1) * BLOCK)
+            index, hot, got, local_u, local_v = kept[b]
+            weight_high = high_ref[:, cut]
+            weight_low = low_ref[:, cut]
+            weight = weight_high.astype(F32) + weight_low.astype(F32)
+            slope = red * got[6] + green * got[7] + blue * got[8]
             moved = slope * weight
             rest = whole - prefix(moved, upto)
             whole = rest[:, BLOCK - 1 :]
-            push = moved - rest * (alpha / (1.0 - alpha))
+            push = moved - rest * ratio_ref[:, cut]
             high, low = split(push, 2)
             moment = jnp.dot(power, high, preferred_element_type=F32) + jnp.dot(
                 power, low, preferred_element_type=F32
             )
-            high, low = split(weight, 2)
-            hue = (
-                jnp.dot(res_high, high, preferred_element_type=F32)
-                + jnp.dot(res_low, high, preferred_element_type=F32)
-                + jnp.dot(res_high, low, preferred_element_type=F32)
-            )
+            part = jnp.dot(res_both, weight_high, preferred_element_type=F32)
+            hue = part[0:8] + part[8:16]
+            hue = hue + jnp.dot(res_high, weight_low, preferred_element_type=F32)
             m_0, m_x, m_y, m_xx, m_xy, m_yy = [moment[k : k + 1] for k in range(6)]
             s_x = local_u * m_0 - m_x
             s_y = local_v * m_0 - m_y
@@ -452,10 +486,18 @@
                 ],
                 axis=0,
             )
-            total_ref[...] += scatter_columns(back, index, groups)
-        return carry
-
-    lax.fori_loop(0, tiles, tile, 0)
+            total_ref[...] += scatter_columns(back, index, hot, groups // 2)
+
+    together = 2 - tiles % 2
+
+    def some_tiles(i, carry):
+        states = [front(together * i + slot, slot) for slot in range(together)]
+        for slot in range(together):
+            rear(together * i + slot, slot, *states[slot])
+        return carry
+
+    lax.fori_loop(0, tiles // together, some_tiles, 0)
+    store_lines(out_ref, total_ref[...])
 
 
 def update_kernel(
@@ -507,6 +549,16 @@
         new_params_ref[:, cut] = params_ref[:, cut] - rate * first / (
             jnp.sqrt(second * fix_two) + ADAM_EPSILON
         )
+
+
+def render_scratch(heard, length):
+    return [
+        pltpu.VMEM((SCREEN * heard // 2, WIDE), F32),
+        pltpu.VMEM(((SCREEN + 2) * heard // 2, 2 * WIDE), BF16),
+        pltpu.VMEM((256, 2 * length), BF16),
+        pltpu.VMEM((256, 2 * length), BF16),
+        pltpu.VMEM((256, 2 * length), F32),
+    ]
 
 
 def body(params, adam_m, adam_v, camera, target, tile_ids, tile_blocks, tile_lists, send_rows):
@@ -555,7 +607,7 @@
         in_specs=[vmem, vmem],
         out_specs=vmem,
         out_shape=listed,
-        scratch_shapes=[pltpu.VMEM((SCREEN * groups, 3 * LANES), BF16)] + move_scratch,
+        scratch_shapes=[pltpu.VMEM(((SCREEN + 2) * groups // 2, 2 * WIDE), BF16)] + move_scratch,
         compiler_params=moving(0),
         name="pick_and_send",
     )(screen, rows)
@@ -564,11 +616,7 @@
         in_specs=[vmem, vmem, vmem, smem, smem],
         out_specs=vmem,
         out_shape=listed,
-        scratch_shapes=[
-            pltpu.VMEM((SCREEN * heard, 3 * LANES), BF16),
-            pltpu.VMEM((256, length), F32),
-            pltpu.VMEM((256, length), F32),
-        ],
+        scratch_shapes=render_scratch(heard, length),
         compiler_params=limits,
         name="render_and_back",
     )(arrived, tile_lists, target, tile_ids, tile_blocks)
@@ -577,7 +625,7 @@
         in_specs=[vmem, vmem],
         out_specs=vmem,
         out_shape=owned,
-        scratch_shapes=move_scratch,
+        scratch_shapes=[pltpu.VMEM((SCREEN * groups // 2, WIDE), F32)] + move_scratch,
         compiler_params=moving(1),
         name="return_and_add",
     )(slopes, rows)

time: 98.9 us -> 92.9 us (0.939)
  Pallas kernels: 95.5 us -> 89.4 us
    pallas_call x1, Pallas kernels: 40.7 us -> 36.3 us  [body(): pl.pallas_call(functools.partial(render_kernel, (heard, tiles, length)),...]
    pallas_call x1, Pallas kernels: 19.7 us -> 17.9 us  [body(): pl.pallas_call(functools.partial(send_kernel, move_sizes), in_specs=[vmem...]
where the time goes in v3:
time: 92.9 us; the launch traced here: 91.4 us
  Pallas kernels  89.4 us (96%)
  local copies, waits for them, and re-layouts  1.37 us (1%)
    pallas_call x1, Pallas kernels, body(): pl.pallas_call(functools.partial(render_kernel, (heard, tiles, length)),...  36.3 us
    pallas_call x1, Pallas kernels, body(): pl.pallas_call(functools.partial(return_kernel, move_sizes), in_specs=[vm...  21 us
    pallas_call x1, Pallas kernels, body(): pl.pallas_call(functools.partial(send_kernel, move_sizes), in_specs=[vmem...  17.9 us
    pallas_call x1, Pallas kernels, body(): pl.pallas_call(functools.partial(update_kernel, view_sizes), grid=(steps,...  8.91 us
    pallas_call x1, Pallas kernels, body(): pl.pallas_call(functools.partial(owner_kernel, view_sizes), grid=(steps,)...  5.29 us

profile of v3, /device:TPU:1, one launch (start us, length us, event | category | flops | bytes accessed | tf_op | source)
XLA Modules:
  0.0 91.4 jit_solution(17673252308581475827)
XLA Ops:
  0.6 1.4 %copy.12.target_ref = f32[8,3,256]{2,1,0:T(4,128)} copy(f32[8,3,256]{2,0,1:T(8,128)} %param.13) | data formatting | bytes 49152 | tf_op args[4]
  2.0 5.3 %project.1.screen_ref = f32[576,128]{1,0:T(8,128)} custom-call(f32[59,8192]{1,0:T(8,128)} %params_ref.3, f32[6]{0:T(128)} %cam_ref.3), custom_call_target="tpu_custom_call" | custom-call | tf_op jit(solution)/shard_map/project/pallas_call | solution.py:595
  7.3 17.9 %pick_and_send.1.lines_ref = f32[576,128]{1,0:T(8,128)} custom-call(f32[576,128]{1,0:T(8,128)} %project.1.screen_ref, s32[16,512]{1,0:T(8,128)} %bitcast.1), custom_call_target="tpu_custom_call" | custom-call | tf_op jit(solution)/shard_map/pick_and_send/pallas_call | solution.py:605
  25.2 36.3 %render_and_back.1.slopes_ref = f32[576,128]{1,0:T(8,128)} custom-call(f32[576,128]{1,0:T(8,128)} %pick_and_send.1.lines_ref, s32[8,1024]{1,0:T(8,128)} %lists_ref.1, f32[8,3,256]{2,1,0:T(4,128)} %copy.12.target_ref, s32[8]{0:T(128)} %ids_ref.1, s32[8]{0:T(128)} %blocks_ref.1), custom_call_target="tpu_custom_call" | custom-call | tf_op jit(solution)/shard_map/render_and_back/pallas_call | solution.py:614
  61.5 21.0 %return_and_add.1.total_ref = f32[576,128]{1,0:T(8,128)} custom-call(f32[576,128]{1,0:T(8,128)} %render_and_back.1.slopes_ref, s32[16,512]{1,0:T(8,128)} %bitcast.2), custom_call_target="tpu_custom_call" | custom-call | tf_op jit(solution)/shard_map/return_and_add/pallas_call | solution.py:623
  82.5 8.9 %gradient_and_step.1 = (f32[59,8192]{1,0:T(8,128)}, f32[59,8192]{1,0:T(8,128)}, f32[59,8192]{1,0:T(8,128)}) custom-call(f32[59,8192]{1,0:T(8,128)} %params_ref.3, f32[59,8192]{1,0:T(8,128)} %m_ref.1, f32[59,8192]{1,0:T(8,128)} %v_ref.1, f32[6]{0:T(128)} %cam_ref.3, f32[576,128]{1,0:T(8,128)} %return_and_add.1.total_ref), custom_call_target="tpu_custom_call" | custom-call | tf_op jit(solution)/shard_map/gradient_and_step/pallas_call | solution.py:633
